TPU v7x, 512 devices: a whole 4x4x16 slice. The times are simulated.
512 devices in a mesh: blk: 32 (over z_hi, y, core), freq: 16 (over x, z_lo).
Axes of the slice: x: 4, y: 4, z: 16 (z_hi: 4, z_lo: 4; z = z_hi * 4 + z_lo), core: 2. Of those that a mesh axis runs over, the one named last changes fastest.
Arguments:
- spectra: bfloat16 [2, 8, 2048, 2048], P(None, None, 'blk', 'freq'), may hold values from -60 to 60
- pairing: int32 [2], replicated, may hold values from 1 to 31, as said below
Outputs:
- lags: float32 [2, 256, 131072], P(None, 'freq', 'blk')
Inputs may be any that keep to these rules, and one draw needn't show every extreme that they name: The values of different rounds differ; round r pairs block b with block b XOR pairing[r]; some round holds 31.
All inputs are finite; a program needn't handle non-finite values.
Results may differ from a plain program's by a relative error of at most 0.025.
Values may be sent and summed in bfloat16 or wider, within the bound.
A program may use at most 64 MiB of HBM per device.

v0:
```python
import math

import jax
import jax.numpy as jnp
from jax import lax
from jax.sharding import PartitionSpec as P

NB = 2048
L = 256


epsilon = 1e-06


def from_partner(block, axis, bit):
    count = lax.axis_size(axis)
    route = []
    for low in range(count):
        high = low | 1 << bit
        if high != low and high < count:
            route += [(low, high), (high, low)]
    return lax.ppermute(block, axis, route)


def phase_tables(bin_first, bin_total, lag_total, bin_count):
    bin_index = bin_first + jnp.arange(bin_count, dtype=jnp.int32)
    lag_index = jnp.arange(lag_total, dtype=jnp.int32) - lag_total // 2
    phase_steps = jnp.mod(lag_index[:, None] * bin_index[None, :], 2 * bin_total)
    phase_angle = phase_steps.astype(jnp.float32) * (math.pi / bin_total)
    return jnp.stack([jnp.cos(phase_angle), -jnp.sin(phase_angle)], axis=1)


def whiten(spectra):
    values = spectra.astype(jnp.float32)
    windows = spectra.shape[1]
    chan_power = jnp.sum(values * values, axis=(0, 1)) / windows
    return (values / jnp.sqrt(chan_power + epsilon)).astype(jnp.bfloat16)


def pair_spectrum(own_stack, partner, windows):
    block_width = partner.shape[2]
    bin_count = partner.shape[3]
    real_side = jnp.concatenate([partner[0], partner[1]], axis=0)
    imag_side = jnp.concatenate([partner[1], -partner[0]], axis=0)
    partner_stack = jnp.concatenate([real_side, imag_side], axis=1)
    spectrum = jnp.einsum(
        "wif,wkf->fik", own_stack, partner_stack, preferred_element_type=jnp.float32
    ) / math.sqrt(windows)
    spectrum = spectrum.astype(jnp.bfloat16).reshape(bin_count, block_width, 2, block_width)
    spectrum = spectrum.transpose(2, 0, 1, 3)
    return spectrum.reshape(2 * bin_count, block_width * block_width)


def on_device(spectra, pairing):
    windows = spectra.shape[1]
    bin_count = spectra.shape[3]
    rounds = pairing.shape[0]
    white = whiten(spectra)
    own_stack = jnp.concatenate([white[0], white[1]], axis=0)
    bit_count = lax.axis_size("blk").bit_length() - 1
    bit_sequence = list(range(bit_count))
    partners = []
    for round_index in range(rounds):
        current = white
        for bit_index in bit_sequence:
            swapped = from_partner(current, "blk", bit_index)
            current = jnp.where(
                jnp.right_shift(pairing[round_index], bit_index) % 2 == 1, swapped, current
            )
        partners.append(current)
    lag_table = (
        phase_tables(lax.axis_index("freq") * bin_count, NB, L, bin_count)
        .reshape(L, 2 * bin_count)
        .astype(jnp.bfloat16)
    )
    lag_share = L // lax.axis_size("freq")
    results = []
    for round_index in range(rounds):
        spectrum = pair_spectrum(own_stack, partners[round_index], windows)

        def lag_term(first_row, row_count, spectrum=spectrum):
            return jnp.dot(lag_table, spectrum, preferred_element_type=jnp.float32) / math.sqrt(NB)

        results.append(
            lax.psum_scatter(
                lag_term(jnp.int32(0), lag_share * lax.axis_size("freq")).astype(jnp.bfloat16),
                "freq",
                scatter_dimension=0,
                tiled=True,
            ).astype(jnp.float32)
        )
    return jnp.stack(results)


def solution(mesh):
    in_specs = (P(None, None, "blk", "freq"), P())
    out_specs = P(None, "freq", "blk")
    return jax.shard_map(
        on_device, mesh=mesh, in_specs=in_specs, out_specs=out_specs, check_vma=False
    )
```

profile of v0, /device:TPU:16, one launch (start us, length us, event | category | flops | bytes accessed | tf_op | source)
XLA Modules:
  0.0 421.5 jit_solution(16196697025607422626)
XLA Ops:
  6.5 1.3 copy.15
  8.2 1.9 collective-permute-start
  10.2 0.6 fusion.29
  12.1 0.3 broadcast_select_fusion.5
  12.4 3.2 collective-permute-start.1
  16.2 12.4 %collective-permute-done.1 = bf16[2,8,64,128]{2,1,3,0:T(8,128)(2,1)S(1)} collective-permute-done((bf16[2,8,64,128]{2,1,3,0:T(8,128)(2,1)S(1)}, bf16[2,8,64,128]{2,1,3,0:T(8,128)(2,1)S(1)}, u32[]{:S(2)}, u32[]{:S(2)}) %collective-permute-start.1) | collective-permute-done | bytes 262176 | tf_op jit(solution)/shard_map/ppermute | solution.py:22
  28.7 7.6 %collective-permute-start.2 = (bf16[2,8,64,128]{2,1,3,0:T(8,128)(2,1)S(1)}, bf16[2,8,64,128]{2,1,3,0:T(8,128)(2,1)S(1)}, u32[]{:S(2)}, u32[]{:S(2)}) collective-permute-start(bf16[2,8,64,128]{2,1,3,0:T(8,128)(2,1)S(1)} %broadcast_select_fusion.6), channel_id=1, source_target_pairs={{0,64},{64,0},{16,80},{80,16},{32,96},{96,32},{48,112},{112,48},{1... | collective-permute-start | bytes 786440 | tf_op jit(solution)/shard_map/ppermute | solution.py:22
  37.0 11.1 %collective-permute-done.2 = bf16[2,8,64,128]{2,1,3,0:T(8,128)(2,1)S(1)} collective-permute-done((bf16[2,8,64,128]{2,1,3,0:T(8,128)(2,1)S(1)}, bf16[2,8,64,128]{2,1,3,0:T(8,128)(2,1)S(1)}, u32[]{:S(2)}, u32[]{:S(2)}) %collective-permute-start.2) | collective-permute-done | bytes 262176 | tf_op jit(solution)/shard_map/ppermute | solution.py:22
  48.1 6.6 %collective-permute-start.3 = (bf16[2,8,64,128]{2,1,3,0:T(8,128)(2,1)S(1)}, bf16[2,8,64,128]{2,1,3,0:T(8,128)(2,1)S(1)}, u32[]{:S(2)}, u32[]{:S(2)}) collective-permute-start(bf16[2,8,64,128]{2,1,3,0:T(8,128)(2,1)S(1)} %broadcast_select_fusion.7), channel_id=1, source_target_pairs={{0,128},{128,0},{16,144},{144,16},{32,160},{160,32},{48,176},{176,... | collective-permute-start | bytes 786440 | tf_op jit(solution)/shard_map/ppermute | solution.py:22
  55.4 0.6 cosine_convert_fusion
  56.0 44.6 %collective-permute-done.3 = bf16[2,8,64,128]{2,1,3,0:T(8,128)(2,1)S(1)} collective-permute-done((bf16[2,8,64,128]{2,1,3,0:T(8,128)(2,1)S(1)}, bf16[2,8,64,128]{2,1,3,0:T(8,128)(2,1)S(1)}, u32[]{:S(2)}, u32[]{:S(2)}) %collective-permute-start.3) | collective-permute-done | bytes 262176 | tf_op jit(solution)/shard_map/ppermute | solution.py:22
  100.7 24.3 %collective-permute-start.4 = (bf16[2,8,64,128]{2,1,3,0:T(8,128)(2,1)S(1)}, bf16[2,8,64,128]{2,1,3,0:T(8,128)(2,1)S(1)}, u32[]{:S(2)}, u32[]{:S(2)}) collective-permute-start(bf16[2,8,64,128]{2,1,3,0:T(8,128)(2,1)S(1)} %broadcast_select_fusion.8), channel_id=1, source_target_pairs={{0,256},{256,0},{16,272},{272,16},{32,288},{288,32},{48,304},{304,... | collective-permute-start | bytes 786440 | tf_op jit(solution)/shard_map/ppermute | solution.py:22
  125.8 20.0 %collective-permute-done.4 = bf16[2,8,64,128]{2,1,3,0:T(8,128)(2,1)S(1)} collective-permute-done((bf16[2,8,64,128]{2,1,3,0:T(8,128)(2,1)S(1)}, bf16[2,8,64,128]{2,1,3,0:T(8,128)(2,1)S(1)}, u32[]{:S(2)}, u32[]{:S(2)}) %collective-permute-start.4) | collective-permute-done | bytes 262176 | tf_op jit(solution)/shard_map/ppermute | solution.py:22
  146.0 2.4 multiply_convert_fusion.1
  148.4 3.3 copy.16
  151.7 2.2 copy.17
  153.8 2.1 fusion
  156.0 3.2 collective-permute-start.5
  159.9 11.6 %collective-permute-done.5 = bf16[2,8,64,128]{2,1,3,0:T(8,128)(2,1)S(1)} collective-permute-done((bf16[2,8,64,128]{2,1,3,0:T(8,128)(2,1)S(1)}, bf16[2,8,64,128]{2,1,3,0:T(8,128)(2,1)S(1)}, u32[]{:S(2)}, u32[]{:S(2)}) %collective-permute-start.5) | collective-permute-done | bytes 262176 | tf_op jit(solution)/shard_map/ppermute | solution.py:22
  171.5 2.2 collective-permute-start.6
  174.4 13.2 %collective-permute-done.6 = bf16[2,8,64,128]{2,1,3,0:T(8,128)(2,1)S(1)} collective-permute-done((bf16[2,8,64,128]{2,1,3,0:T(8,128)(2,1)S(1)}, bf16[2,8,64,128]{2,1,3,0:T(8,128)(2,1)S(1)}, u32[]{:S(2)}, u32[]{:S(2)}) %collective-permute-start.6) | collective-permute-done | bytes 262176 | tf_op jit(solution)/shard_map/ppermute | solution.py:22
  187.7 12.7 %collective-permute-start.7 = (bf16[2,8,64,128]{2,1,3,0:T(8,128)(2,1)S(1)}, bf16[2,8,64,128]{2,1,3,0:T(8,128)(2,1)S(1)}, u32[]{:S(2)}, u32[]{:S(2)}) collective-permute-start(bf16[2,8,64,128]{2,1,3,0:T(8,128)(2,1)S(1)} %broadcast_select_fusion.2), channel_id=1, source_target_pairs={{0,128},{128,0},{16,144},{144,16},{32,160},{160,32},{48,176},{176,... | collective-permute-start | bytes 786440 | tf_op jit(solution)/shard_map/ppermute | solution.py:22
  201.0 27.0 %collective-permute-done.7 = bf16[2,8,64,128]{2,1,3,0:T(8,128)(2,1)S(1)} collective-permute-done((bf16[2,8,64,128]{2,1,3,0:T(8,128)(2,1)S(1)}, bf16[2,8,64,128]{2,1,3,0:T(8,128)(2,1)S(1)}, u32[]{:S(2)}, u32[]{:S(2)}) %collective-permute-start.7) | collective-permute-done | bytes 262176 | tf_op jit(solution)/shard_map/ppermute | solution.py:22
  228.1 6.0 %collective-permute-start.8 = (bf16[2,8,64,128]{2,1,3,0:T(8,128)(2,1)S(1)}, bf16[2,8,64,128]{2,1,3,0:T(8,128)(2,1)S(1)}, u32[]{:S(2)}, u32[]{:S(2)}) collective-permute-start(bf16[2,8,64,128]{2,1,3,0:T(8,128)(2,1)S(1)} %broadcast_select_fusion.3), channel_id=1, source_target_pairs={{0,256},{256,0},{16,272},{272,16},{32,288},{288,32},{48,304},{304,... | collective-permute-start | bytes 786440 | tf_op jit(solution)/shard_map/ppermute | solution.py:22
  234.7 52.5 %collective-permute-done.8 = bf16[2,8,64,128]{2,1,3,0:T(8,128)(2,1)S(1)} collective-permute-done((bf16[2,8,64,128]{2,1,3,0:T(8,128)(2,1)S(1)}, bf16[2,8,64,128]{2,1,3,0:T(8,128)(2,1)S(1)}, u32[]{:S(2)}, u32[]{:S(2)}) %collective-permute-start.8) | collective-permute-done | bytes 262176 | tf_op jit(solution)/shard_map/ppermute | solution.py:22
  287.4 2.4 multiply_convert_fusion
  289.8 3.3 copy.18
  293.1 2.2 copy.19
  295.3 2.1 fusion.1
  297.4 11.6 %reduce-scatter.3.cloned.1.call-done = bf16[16,4096]{1,0:T(8,128)(2,1)} async-done(((bf16[256,4096]{1,0:T(8,128)(2,1)}), bf16[16,4096]{1,0:T(8,128)(2,1)}) %reduce-scatter.3.cloned.1.call-update) | async-done | bytes 131088 | tf_op jit(solution)/shard_map/reduce_scatter | solution.py:85
  309.0 103.9 %reduce-scatter.5.cloned.1.call-done = bf16[16,4096]{1,0:T(8,128)(2,1)} async-done(((bf16[256,4096]{1,0:T(8,128)(2,1)}), bf16[16,4096]{1,0:T(8,128)(2,1)}) %reduce-scatter.5.cloned.1.call-update) | async-done | bytes 131088 | tf_op jit(solution)/shard_map/reduce_scatter | solution.py:85
  412.8 1.8 maximum_convert_fusion
  (27 shorter events, 1.2 us)
Async XLA Ops:
  6.5 3.6 copy-start
  6.5 302.4 %reduce-scatter.3.cloned.1.call-start = ((), (), s32[]{:S(2)}) async-start(), calls=%async_computation.2 | async-start | bytes 2228224 | tf_op jit(solution)/shard_map/reduce_scatter | solution.py:85
  8.2 3.9 collective-permute-start
  12.4 16.2 %collective-permute-start.1 = (bf16[2,8,64,128]{2,1,3,0:T(8,128)(2,1)S(1)}, bf16[2,8,64,128]{2,1,3,0:T(8,128)(2,1)S(1)}, u32[]{:S(2)}, u32[]{:S(2)}) collective-permute-start(bf16[2,8,64,128]{2,1,3,0:T(8,128)(2,1)S(1)} %get-tuple-element.5), channel_id=1, source_target_pairs={{0,32},{32,0},{16,48},{48,16},{64,96},{96,64},{80,112},{112,80},{1... | collective-permute-start | bytes 786440 | tf_op jit(solution)/shard_map/ppermute | solution.py:22
  28.7 19.4 %collective-permute-start.2 = (bf16[2,8,64,128]{2,1,3,0:T(8,128)(2,1)S(1)}, bf16[2,8,64,128]{2,1,3,0:T(8,128)(2,1)S(1)}, u32[]{:S(2)}, u32[]{:S(2)}) collective-permute-start(bf16[2,8,64,128]{2,1,3,0:T(8,128)(2,1)S(1)} %broadcast_select_fusion.6), channel_id=1, source_target_pairs={{0,64},{64,0},{16,80},{80,16},{32,96},{96,32},{48,112},{112,48},{1... | collective-permute-start | bytes 786440 | tf_op jit(solution)/shard_map/ppermute | solution.py:22
  48.1 52.5 %collective-permute-start.3 = (bf16[2,8,64,128]{2,1,3,0:T(8,128)(2,1)S(1)}, bf16[2,8,64,128]{2,1,3,0:T(8,128)(2,1)S(1)}, u32[]{:S(2)}, u32[]{:S(2)}) collective-permute-start(bf16[2,8,64,128]{2,1,3,0:T(8,128)(2,1)S(1)} %broadcast_select_fusion.7), channel_id=1, source_target_pairs={{0,128},{128,0},{16,144},{144,16},{32,160},{160,32},{48,176},{176,... | collective-permute-start | bytes 786440 | tf_op jit(solution)/shard_map/ppermute | solution.py:22
  100.7 45.2 %collective-permute-start.4 = (bf16[2,8,64,128]{2,1,3,0:T(8,128)(2,1)S(1)}, bf16[2,8,64,128]{2,1,3,0:T(8,128)(2,1)S(1)}, u32[]{:S(2)}, u32[]{:S(2)}) collective-permute-start(bf16[2,8,64,128]{2,1,3,0:T(8,128)(2,1)S(1)} %broadcast_select_fusion.8), channel_id=1, source_target_pairs={{0,256},{256,0},{16,272},{272,16},{32,288},{288,32},{48,304},{304,... | collective-permute-start | bytes 786440 | tf_op jit(solution)/shard_map/ppermute | solution.py:22
  156.0 256.9 %reduce-scatter.5.cloned.1.call-start = ((), (), s32[]{:S(2)}) async-start(), calls=%async_computation.3 | async-start | bytes 2228224 | tf_op jit(solution)/shard_map/reduce_scatter | solution.py:85
  156.0 15.4 %collective-permute-start.5 = (bf16[2,8,64,128]{2,1,3,0:T(8,128)(2,1)S(1)}, bf16[2,8,64,128]{2,1,3,0:T(8,128)(2,1)S(1)}, u32[]{:S(2)}, u32[]{:S(2)}) collective-permute-start(bf16[2,8,64,128]{2,1,3,0:T(8,128)(2,1)S(1)} %get-tuple-element.6), channel_id=1, source_target_pairs={{0,32},{32,0},{16,48},{48,16},{64,96},{96,64},{80,112},{112,80},{1... | collective-permute-start | bytes 786440 | tf_op jit(solution)/shard_map/ppermute | solution.py:22
  171.5 16.1 %collective-permute-start.6 = (bf16[2,8,64,128]{2,1,3,0:T(8,128)(2,1)S(1)}, bf16[2,8,64,128]{2,1,3,0:T(8,128)(2,1)S(1)}, u32[]{:S(2)}, u32[]{:S(2)}) collective-permute-start(bf16[2,8,64,128]{2,1,3,0:T(8,128)(2,1)S(1)} %broadcast_select_fusion.1), channel_id=1, source_target_pairs={{0,64},{64,0},{16,80},{80,16},{32,96},{96,32},{48,112},{112,48},{1... | collective-permute-start | bytes 786440 | tf_op jit(solution)/shard_map/ppermute | solution.py:22
  187.7 40.3 %collective-permute-start.7 = (bf16[2,8,64,128]{2,1,3,0:T(8,128)(2,1)S(1)}, bf16[2,8,64,128]{2,1,3,0:T(8,128)(2,1)S(1)}, u32[]{:S(2)}, u32[]{:S(2)}) collective-permute-start(bf16[2,8,64,128]{2,1,3,0:T(8,128)(2,1)S(1)} %broadcast_select_fusion.2), channel_id=1, source_target_pairs={{0,128},{128,0},{16,144},{144,16},{32,160},{160,32},{48,176},{176,... | collective-permute-start | bytes 786440 | tf_op jit(solution)/shard_map/ppermute | solution.py:22
  228.1 59.2 %collective-permute-start.8 = (bf16[2,8,64,128]{2,1,3,0:T(8,128)(2,1)S(1)}, bf16[2,8,64,128]{2,1,3,0:T(8,128)(2,1)S(1)}, u32[]{:S(2)}, u32[]{:S(2)}) collective-permute-start(bf16[2,8,64,128]{2,1,3,0:T(8,128)(2,1)S(1)} %broadcast_select_fusion.3), channel_id=1, source_target_pairs={{0,256},{256,0},{16,272},{272,16},{32,288},{288,32},{48,304},{304,... | collective-permute-start | bytes 786440 | tf_op jit(solution)/shard_map/ppermute | solution.py:22
Sparse Core Ops, SparseCore 0:
  156.1 152.8 reduce-scatter.2
  311.8 101.0 reduce-scatter.4
where the time goes:
time: 422 us; the launch traced here: 421 us
  waiting for transfers between devices  308 us (73%)
  starting transfers between devices  67.9 us (16%)
  between operations  20.2 us (5%)
  local copies, waits for them, and re-layouts  13 us (3%)
  matrix products  8.96 us (2%)
    ppermute x9, waiting for transfers between devices, from_partner(): return lax.ppermute(block, axis, route)  192 us
    reduce_scatter x2, waiting for transfers between devices, on_device(): lax.psum_scatter(lag_term(jnp.int32(0), lag_share * lax.axis_size('freq')...  115 us
    ppermute x9, starting transfers between devices, from_partner(): return lax.ppermute(block, axis, route)  67.8 us
  transfers between devices with their start and end apart: 11, of which 10 were waited for; matrix products, arithmetic and copies ran while one was open for 3% of the time, Pallas kernels for 0%

commit v1 on v0

v1 whole, which is shorter than its diff:
```python
import functools
import math

import jax
import jax.numpy as jnp
from jax import lax
from jax.experimental import pallas as pl
from jax.experimental.pallas import tpu as pltpu
from jax.sharding import PartitionSpec as P

NB = 2048
L = 256
EPS = 1e-06
MESH = pl.DeviceIdType.MESH
ROWS = 272
CK = 4
f32, bf16 = jnp.float32, jnp.bfloat16


def xor(v, mask):
    out = v
    for k in range(5):
        if mask >> k & 1:
            out = out + (1 - 2 * ((v // (1 << k)) % 2)) * (1 << k)
    return out


def phase_table(first, count):
    bins = first + jnp.arange(count, dtype=jnp.int32)
    lags = jnp.arange(ROWS, dtype=jnp.int32) - L // 2
    steps = jnp.mod(lags[:, None] * bins[None, :], 2 * NB)
    angle = steps.astype(f32) * (math.pi / NB)
    return jnp.concatenate([jnp.cos(angle), -jnp.sin(angle)], axis=1).astype(bf16)


def whiten(spectra):
    values = spectra.astype(f32)
    power = jnp.sum(values * values, axis=(0, 1)) / spectra.shape[1]
    return (values / jnp.sqrt(power + EPS)).astype(bf16)


def roles(p, blk):
    low = (p & -p).bit_length() - 1
    return blk % 2, (blk // (1 << low)) % 2


def moves(sends, recvs, locals_, ss, rs):
    barrier = pltpu.get_barrier_semaphore()
    for _, _, source in recvs:
        pl.semaphore_signal(barrier, inc=1, device_id=source, device_id_type=MESH)
    pl.semaphore_wait(barrier, len(sends))
    copies = []
    for n, (src, dst, slot, target) in enumerate(sends):
        copy = pltpu.make_async_remote_copy(
            src_ref=src, dst_ref=dst, send_sem=ss.at[n], recv_sem=rs.at[slot],
            device_id=target, device_id_type=MESH)
        copy.start()
        copies.append(copy)
    for src, dst in locals_:
        dst[...] = src[...]
    for copy in copies:
        copy.wait_send()
    for dst, slot, source in recvs:
        pltpu.make_async_remote_copy(
            src_ref=dst, dst_ref=dst, send_sem=ss.at[0], recv_sem=rs.at[slot],
            device_id=source, device_id_type=MESH).wait_recv()


def exchange_kernel(p, w, m1, m2, ss, rs):
    blk, h = lax.axis_index("blk"), lax.axis_index("freq")
    core, role = roles(p, blk)
    to = lambda mask: (xor(blk, mask), h)
    one = functools.partial(moves, ss=ss, rs=rs)
    if p % 2:
        @pl.when(core == 0)
        def _():
            one([(w, m2, 1, to(p))], [(m2, 1, to(31))], [(w, m1)])

        @pl.when(core == 1)
        def _():
            one([(w, m2, 1, to(31))], [(m2, 1, to(p))], [(w, m1)])
    else:
        @pl.when((core == 0) & (role == 0))
        def _():
            one([(w, m2, 1, to(p ^ 1))], [(m2, 1, to(31))], [(w, m1)])

        @pl.when((core == 0) & (role == 1))
        def _():
            one([(w, m1, 0, to(1))], [(m2, 1, to(31))], [(w, m1)])

        @pl.when((core == 1) & (role == 0))
        def _():
            one([(w, m2, 1, to(31))], [(m2, 1, to(p))], [(w, m1)])

        @pl.when((core == 1) & (role == 1))
        def _():
            one([(w, m2, 1, to(31)), (w, m2, 1, to(p))],
                [(m1, 0, to(1)), (m2, 1, to(p ^ 1))], [])


def result_kernel(p, f, row, za, zb, ra, rb, ss, rs):
    blk, h = lax.axis_index("blk"), lax.axis_index("freq")
    core, role = roles(p, blk)
    flip, turn = 15 - h, (16 - h) % 16
    one = functools.partial(moves, ss=ss, rs=rs)

    def mirror(z, r, slot, mask):
        peer = xor(blk, mask)
        return ([(f, z, slot, (peer, flip)), (row, r, slot + 2, (peer, turn))],
                [(z, slot, (peer, flip)), (r, slot + 2, (peer, turn))])

    a_send, a_recv = mirror(za, ra, 0, 31)
    b_send, b_recv = mirror(zb, rb, 1, p)
    own_a, own_b = [(f, za), (row, ra)], [(f, zb), (row, rb)]
    if p % 2:
        @pl.when(core == 0)
        def _():
            one(a_send, b_recv, own_a)

        @pl.when(core == 1)
        def _():
            one(b_send, a_recv, own_b)
    else:
        c_send, c_recv = mirror(zb, rb, 1, p ^ 1)
        beside = (xor(blk, 1), h)

        @pl.when((core == 0) & (role == 0))
        def _():
            one(a_send, c_recv, own_a)

        @pl.when((core == 0) & (role == 1))
        def _():
            one(a_send, [(zb, 1, beside)], own_a + [(row, rb)])

        @pl.when((core == 1) & (role == 0))
        def _():
            one(b_send, a_recv, own_b)

        @pl.when((core == 1) & (role == 1))
        def _():
            one(c_send + [(f, zb, 1, beside)], a_recv + b_recv, [])


def remote_call(kernel, p, cid, name, shapes, n_send, n_recv, *args):
    spec = pl.BlockSpec(memory_space=pltpu.VMEM)
    return pl.pallas_call(
        functools.partial(kernel, p),
        out_shape=[jax.ShapeDtypeStruct(s, bf16) for s in shapes],
        in_specs=[spec] * len(args),
        out_specs=[spec] * len(shapes),
        scratch_shapes=[pltpu.SemaphoreType.DMA((n_send,)), pltpu.SemaphoreType.DMA((n_recv,))],
        compiler_params=pltpu.CompilerParams(
            collective_id=cid, has_side_effects=True, vmem_limit_bytes=16 << 20),
        name=name,
    )(*args)


def lag_kernel(m1, m2, table, out, row_out, a32, x_buf, part, extra, fwd, rx, summed, rz,
               e_send, e_rx, e_mid, e_rz, ss, fs, rs, zs, zr, es, er, fin):
    blk, h = lax.axis_index("blk"), lax.axis_index("freq")
    x, z = h // 4, h % 4
    xr, xl, xo = (x + 1) % 4, (x + 3) % 4, (x + 2) % 4
    at_x = lambda v: (blk, v * 4 + z)
    zp = [(z + k) % 4 for k in (1, 2, 3)]
    at_z = lambda v: (blk, x * 4 + v)

    barrier = pltpu.get_barrier_semaphore()
    for peer in [at_x(xr), at_x(xl), at_x(xo)] + [at_z(v) for v in zp]:
        pl.semaphore_signal(barrier, inc=1, device_id=peer, device_id_type=MESH)

    a32[...] = m1[...].astype(f32)

    def quad(n, ck, half):
        for ii in range(4):
            i = n * 4 + ii
            rows = [[jnp.broadcast_to(a32[c, w, pl.ds(i, 1), :], (16, 128)).astype(bf16)
                     for w in range(8)] for c in range(2)]
            for jt in range(4):
                js = pl.ds(jt * 16, 16)
                re, im = [], []
                for w in range(8):
                    a0, a1 = rows[0][w], rows[1][w]
                    b0, b1 = m2[0, w, js, :], m2[1, w, js, :]
                    re.append(a0 * b0 + a1 * b1)
                    im.append(a0 * b1 - a1 * b0)
                while len(re) > 1:
                    re = [re[k] + re[k + 1] for k in range(0, len(re), 2)]
                    im = [im[k] + im[k + 1] for k in range(0, len(im), 2)]
                x_buf[pl.ds(ii * 64 + jt * 16, 16), 0:128] = re[0]
                x_buf[pl.ds(ii * 64 + jt * 16, 16), 128:256] = im[0]
        prod = lax.dot_general(table[...], x_buf[...], (((1,), (1,)), ((), ())),
                               preferred_element_type=f32) * (1.0 / 128.0)
        cols = pl.ds(pl.multiple_of((n % 2) * 256, 256), 256)
        part[ck, half, :, :, cols] = prod[0:256].astype(bf16).reshape(4, 64, 256)
        for k in range(2):
            extra[pl.ds(2 * n + k, 1), :] = prod[256:257, k * 128:(k + 1) * 128]

    def copy(src, dst, s, r, peer):
        c = pltpu.make_async_remote_copy(src_ref=src, dst_ref=dst, send_sem=s, recv_sem=r,
                                         device_id=peer, device_id_type=MESH)
        c.start()
        return c

    first, second, third = {}, {}, {}

    def stage0(ck):
        for half in range(2):
            def body(q, carry, half=half):
                quad(ck * 4 + half * 2 + q, ck, half)
                return carry
            lax.fori_loop(0, 2, body, 0)
            if ck == 0 and half == 0:
                pl.semaphore_wait(barrier, 6)
            if half == 0:
                first[ck] = [copy(part.at[ck, 0, xo], fwd.at[ck, 0], fs.at[ck, 0], fs.at[ck, 2], at_x(xr)),
                             copy(part.at[ck, 0, xl], rx.at[ck, 1, 0], ss.at[ck, 0], rs.at[ck, 0], at_x(xl))]
            else:
                first[ck] += [copy(part.at[ck, 1, xo], fwd.at[ck, 1], fs.at[ck, 1], fs.at[ck, 3], at_x(xl)),
                              copy(part.at[ck, 1, xr], rx.at[ck, 0, 1], ss.at[ck, 1], rs.at[ck, 1], at_x(xr))]

    def stage1(ck):
        first[ck][0].wait_recv()
        part[ck, 0, xr] = (part[ck, 0, xr].astype(f32) + fwd[ck, 0].astype(f32)).astype(bf16)
        second[ck] = [copy(part.at[ck, 0, xr], rx.at[ck, 0, 0], ss.at[ck, 2], rs.at[ck, 2], at_x(xr))]
        first[ck][2].wait_recv()
        part[ck, 1, xl] = (part[ck, 1, xl].astype(f32) + fwd[ck, 1].astype(f32)).astype(bf16)
        second[ck] += [copy(part.at[ck, 1, xl], rx.at[ck, 1, 1], ss.at[ck, 3], rs.at[ck, 3], at_x(xl))]

    def stage2(ck):
        first[ck][1].wait_recv()
        first[ck][3].wait_recv()
        second[ck][0].wait_recv()
        second[ck][1].wait_recv()
        for half in range(2):
            total = (part[ck, half, x].astype(f32) + rx[ck, 0, half].astype(f32)
                     + rx[ck, 1, half].astype(f32))
            summed[ck, :, :, half * 512:(half + 1) * 512] = total.astype(bf16).reshape(4, 16, 512)
        third[ck] = [copy(summed.at[ck, zp[k]], rz.at[ck, 2 - k], zs.at[ck, k], zr.at[ck, 2 - k], at_z(zp[k]))
                     for k in range(3)]

    def stage3(ck):
        for c in third[ck]:
            c.wait_recv()
        total = (summed[ck, z].astype(f32) + rz[ck, 0].astype(f32) + rz[ck, 1].astype(f32)
                 + rz[ck, 2].astype(f32))
        out[:, ck * 1024:(ck + 1) * 1024] = total.astype(bf16)
        for n in range(8):
            fin[ck * 8 + n:ck * 8 + n + 1, :] = total[0:1, n * 128:(n + 1) * 128]

    for step in range(CK + 3):
        if step < CK:
            stage0(step)
            if step == CK - 1:
                e_send[...] = extra[...].astype(bf16)
                edge = [copy(e_send, e_rx.at[k], es.at[k], er.at[k], at_x(v))
                        for k, v in enumerate((xr, xl, xo))]
        if 0 <= step - 1 < CK:
            stage1(step - 1)
        if 0 <= step - 2 < CK:
            stage2(step - 2)
        if step == CK:
            for c in edge:
                c.wait_recv()
            e_mid[...] = (e_send[...].astype(f32) + e_rx[0].astype(f32) + e_rx[1].astype(f32)
                          + e_rx[2].astype(f32)).astype(bf16)
            edge_z = [copy(e_mid, e_rz.at[2 - k], es.at[3 + k], er.at[3 + 2 - k], at_z(zp[k]))
                      for k in range(3)]
        if 0 <= step - 3 < CK:
            stage3(step - 3)
    for c in edge_z:
        c.wait_recv()
    last = (e_mid[...].astype(f32) + e_rz[0].astype(f32) + e_rz[1].astype(f32)
            + e_rz[2].astype(f32))
    row_out[...] = jnp.where(h == 0, last, fin[...]).astype(bf16)
    for ck in range(CK):
        for c in first[ck] + second[ck] + third[ck]:
            c.wait_send()
    for c in edge + edge_z:
        c.wait_send()


def lag_call(m1, m2, table, cid):
    spec = pl.BlockSpec(memory_space=pltpu.VMEM)
    dma = pltpu.SemaphoreType.DMA
    return pl.pallas_call(
        lag_kernel,
        out_shape=[jax.ShapeDtypeStruct((16, 4096), bf16), jax.ShapeDtypeStruct((32, 128), bf16)],
        in_specs=[spec] * 3,
        out_specs=[spec] * 2,
        scratch_shapes=[
            pltpu.VMEM((2, 8, 64, 128), f32),
            pltpu.VMEM((256, 256), bf16),
            pltpu.VMEM((CK, 2, 4, 64, 512), bf16),
            pltpu.VMEM((32, 128), f32),
            pltpu.VMEM((CK, 2, 64, 512), bf16),
            pltpu.VMEM((CK, 2, 2, 64, 512), bf16),
            pltpu.VMEM((CK, 4, 16, 1024), bf16),
            pltpu.VMEM((CK, 3, 16, 1024), bf16),
            pltpu.VMEM((32, 128), bf16),
            pltpu.VMEM((3, 32, 128), bf16),
            pltpu.VMEM((32, 128), bf16),
            pltpu.VMEM((3, 32, 128), bf16),
            dma((CK, 4)), dma((CK, 4)), dma((CK, 4)), dma((CK, 3)), dma((CK, 3)),
            dma((6,)), dma((6,)),
            pltpu.VMEM((32, 128), f32),
        ],
        compiler_params=pltpu.CompilerParams(
            collective_id=cid, has_side_effects=True, vmem_limit_bytes=32 << 20),
        name="lags",
    )(m1, m2, table)


def transposed(z, row):
    wide = jnp.concatenate([row.reshape(1, 4096), z[:0:-1]], axis=0)
    return wide.reshape(16, 64, 64).transpose(0, 2, 1).reshape(16, 4096)


def on_device(spectra, pairing):
    bins = spectra.shape[3]
    blk, h = lax.axis_index("blk"), lax.axis_index("freq")
    white = whiten(spectra)
    table = phase_table(h * bins, bins)
    other = pairing[0] + pairing[1] - 31
    block = white.shape

    def exchange(p):
        return lambda w: tuple(remote_call(exchange_kernel, p, p - 1, "exchange",
                                           [block, block], 2, 2, w))

    def results(p):
        return lambda f, r: tuple(remote_call(
            result_kernel, p, 30 + p, "results",
            [(16, 4096), (16, 4096), (32, 128), (32, 128)], 3, 4, f, r))

    m1, m2 = lax.switch(other - 1, [exchange(p) for p in range(1, 31)], white)
    final, row = lag_call(m1, m2, table, 30)
    za, zb, ra, rb = lax.switch(other - 1, [results(p) for p in range(1, 31)], final, row)

    core = blk % 2
    low = other & -other
    role = ((blk & low) != 0).astype(jnp.int32)
    plain_a = core == 0
    plain_b = jnp.where(other % 2 == 1, core == 1, core != role)
    out_a = jnp.where(plain_a, za, transposed(za, ra))
    out_b = jnp.where(plain_b, zb, transposed(zb, rb))
    first = pairing[0] == 31
    return jnp.stack([jnp.where(first, out_a, out_b), jnp.where(first, out_b, out_a)]).astype(f32)


def solution(mesh):
    in_specs = (P(None, None, "blk", "freq"), P())
    out_specs = P(None, "freq", "blk")
    return jax.shard_map(
        on_device, mesh=mesh, in_specs=in_specs, out_specs=out_specs, check_vma=False
    )
```

time: 422 us -> 99.9 us (0.24)
  the two profiles are of different devices: /device:TPU:16 before, /device:TPU:1 now
where the time goes in v1:
time: 99.9 us; the launch traced here: 99.7 us
  Pallas kernels  89.4 us (89%)
  local copies, waits for them, and re-layouts  4.96 us (5%)
  other arithmetic  2.76 us (3%)
  between operations  2.25 us (2%)
    pallas_call x2, Pallas kernels, remote_call(): pl.pallas_call(functools.partial(kernel, p), out_shape=[jax.ShapeDtypeStr...  61 us
    pallas_call x1, Pallas kernels, lag_call(): pl.pallas_call(lag_kernel, out_shape=[jax.ShapeDtypeStruct((16, 4096), bf...  28.4 us

profile of v1, /device:TPU:1, one launch (start us, length us, event | category | flops | bytes accessed | tf_op | source)
XLA Modules:
  0.0 99.7 jit_solution(7174854312803669479)
XLA Ops:
  0.0 0.0 copy-start
  0.0 1.3 %fusion.5 = (s32[1]{0:T(128)}, s32[1]{0:T(128)}) fusion(s32[2]{0:T(128)} %param.63), kind=kLoop, calls=%fused_computation.25 | loop fusion | bytes 16 | tf_op jit(solution)/shard_map/slice | solution.py:323
  3.4 1.0 %fusion = f32[64,128]{1,0:T(8,128)S(1)} fusion(bf16[2,8,64,128]{3,2,1,0:T(8,128)(2,1)} %param.62), kind=kLoop, calls=%fused_computation.2 | loop fusion | flops 385024 | bytes 294912 | tf_op jit(solution)/shard_map/reduce_sum | solution.py:38
  4.4 0.0 copy-done
  4.4 0.1 fusion.1
  4.5 30.2 %conditional.2 = ((bf16[2,8,64,128]{3,2,1,0:T(8,128)(2,1)S(1)}, bf16[2,8,64,128]{3,2,1,0:T(8,128)(2,1)S(1)})) conditional(s32[]{:T(128)} %bitcast.1, bf16[2,8,64,128]{3,2,1,0:T(8,128)(2,1)S(1)} %fusion.1, bf16[2,8,64,128]{3,2,1,0:T(8,128)(2,1)S(1)} %fusion.1, bf16[2,8,64,128]{3,2,1,0:T(8,128)(2,1)S(1)} %fusion.1, ...), branch_computations={%region_1.2_spmd, %region_2.3_spmd, %region_3.4_spmd, %region_4.5_... | conditional | bytes 8 | solution.py:335
  4.5 30.2 %exchange.43 = (bf16[2,8,64,128]{3,2,1,0:T(8,128)(2,1)S(1)}, bf16[2,8,64,128]{3,2,1,0:T(8,128)(2,1)S(1)}) custom-call(bf16[2,8,64,128]{3,2,1,0:T(8,128)(2,1)S(1)} %w.13), custom_call_target="tpu_custom_call" | custom-call | tf_op jit(solution)/shard_map/cond/branch_13_fun/exchange/pallas_call | solution.py:146
  34.7 0.6 cosine_convert_fusion
  35.4 28.4 %lags.1 = (bf16[16,4096]{1,0:T(8,128)(2,1)S(1)}, bf16[32,128]{1,0:T(8,128)(2,1)S(1)}) custom-call(bf16[2,8,64,128]{3,2,1,0:T(8,128)(2,1)S(1)} %get-tuple-element.348.m1, bf16[2,8,64,128]{3,2,1,0:T(8,128)(2,1)S(1)} %get-tuple-element.349.m2, bf16[272,256]{1,0:T(8,128)(2,1)S(1)} %pad_maximum_fusion.table), custom_call_target="tpu_custom_call" | custom-call | tf_op jit(solution)/shard_map/lags/pallas_call | solution.py:285
  63.8 31.1 %conditional.3 = ((bf16[16,4096]{1,0:T(8,128)(2,1)S(1)}, bf16[16,4096]{1,0:T(8,128)(2,1)S(1)}, bf16[32,128]{1,0:T(8,128)(2,1)S(1)}, bf16[32,128]{1,0:T(8,128)(2,1)S(1)})) conditional(s32[]{:T(128)} %bitcast.1, (bf16[16,4096]{1,0:T(8,128)(2,1)S(1)}, bf16[32,128]{1,0:T(8,128)(2,1)S(1)}) %lags.1, ...), branch_computations={%region_31.32_spmd, %region_32.33_spmd, %region_33.34_spmd, %regio... | conditional | bytes 8 | solution.py:337
  63.9 30.9 %results.43 = (bf16[16,4096]{1,0:T(8,128)(2,1)S(1)}, bf16[16,4096]{1,0:T(8,128)(2,1)S(1)}, bf16[32,128]{1,0:T(8,128)(2,1)S(1)}, bf16[32,128]{1,0:T(8,128)(2,1)S(1)}) custom-call(bf16[16,4096]{1,0:T(8,128)(2,1)S(1)} %get-tuple-element.308.f, bf16[32,128]{1,0:T(8,128)(2,1)S(1)} %get-tuple-element.309.row), custom_call_target="tpu_custom_call" | custom-call | tf_op jit(solution)/shard_map/cond/branch_13_fun/results/pallas_call | solution.py:146
  95.0 0.9 rev.6
  95.9 0.2 concatenate.22
  96.1 0.2 copy.4
  96.3 0.1 concatenate.88
  96.4 0.1 copy.3
  96.5 0.1 maximum_bitcast_fusion
  96.6 0.3 reshape.101
  96.9 0.9 rev.7
  97.8 0.2 concatenate.25
  98.1 0.2 copy.6
  98.3 0.1 concatenate.87
  98.3 0.1 copy.5
  98.4 0.1 maximum_bitcast_fusion.1
  98.5 0.3 reshape.102
  98.9 0.8 maximum_convert_fusion
  (7 shorter events, 0.1 us)
Async XLA Ops:
  0.0 4.4 %copy-start = (bf16[2,8,64,128]{3,2,1,0:T(8,128)(2,1)S(1)}, bf16[2,8,64,128]{3,2,1,0:T(8,128)(2,1)}, u32[]{:S(2)}) copy-start(bf16[2,8,64,128]{3,2,1,0:T(8,128)(2,1)} %param.62) | copy-start | bytes 786436
